TPU v7x, 32 devices: a whole 2x2x4 slice. The times are simulated.
32 devices in a mesh: prow: 4 (over z), pcol: 8 (over y, x, core).
Axes of the slice: x: 2, y: 2, z: 4, core: 2. Of those that a mesh axis runs over, the one named last changes fastest.
Arguments:
- right_sides: bfloat16 [8, 1, 8, 4, 128, 128], P(None, None, 'pcol', 'prow'), may hold values from -6 to 6
- inverses: bfloat16 [8, 1, 8, 4, 128, 128], P(None, None, 'pcol', 'prow'), as said below
- blocks: bfloat16 [7, 1, 8, 4, 4, 8, 128, 128], P(None, None, 'pcol', None, 'prow'), may hold values from -0.0546875 to 0.0546875
- targets: int32 [7, 1, 8, 4, 4, 8], P(None, None, 'pcol', None, 'prow'), may hold values from 32 to 255, as said below
Outputs:
- solution: bfloat16 [8, 1, 8, 4, 128, 128], P(None, None, 'pcol', 'prow')
Inputs may be any that keep to these rules, and one draw needn't show every extreme that they name: `targets`: entry [l, g, c, s, r, m] is the number of a supernode on a level above l whose number is congruent to r modulo 4; numbers may repeat. `inverses`: each block is well conditioned, with a diagonal near one.
All inputs are finite; a program needn't handle non-finite values.
Results may differ from a plain program's by a relative error of at most 0.007.
Values may be sent and summed in bfloat16 or wider, within the bound.
A program may use at most 128 MiB of HBM per device.

v0:
```python
import functools

import jax
import jax.numpy as jnp
from jax import lax
from jax.experimental import pallas as pl
from jax.experimental.pallas import tpu as pltpu
from jax.sharding import PartitionSpec as P

MESH = pl.DeviceIdType.MESH
CHUNKS = 1
F32 = jnp.float32
BF16 = jnp.bfloat16


def dot_nt(a, b):
    return lax.dot_general(a, b, (((1,), (1,)), ((), ())), preferred_element_type=F32)


def kernel(
    dims,
    table,
    slots,
    rs,
    inv,
    blocks,
    out,
    raw,
    merged,
    xs,
    part_in,
    part_out,
    acc,
    own,
    rst,
    load_sem,
    xsend,
    xrecv,
    psend,
    precv,
):
    levels, rows, cols, nbr, size, rhs = dims
    steps = levels - 1
    per = rows * nbr
    half = rhs // CHUNKS
    r = lax.axis_index("prow")
    c = lax.axis_index("pcol")

    def load(l):
        return pltpu.make_async_copy(blocks.at[l], raw.at[l], load_sem.at[l])

    for l in range(steps):
        load(l).start()

    barrier = pltpu.get_barrier_semaphore()
    for k in range(1, cols):
        pl.semaphore_signal(
            barrier, inc=1, device_id={"pcol": lax.rem(c + k, cols)}, device_id_type=MESH
        )
    for k in range(1, rows):
        pl.semaphore_signal(
            barrier, inc=1, device_id={"prow": lax.rem(r + k, rows)}, device_id_type=MESH
        )

    def x_copy(l, h, k):
        return pltpu.make_async_remote_copy(
            src_ref=xs.at[l, h, r],
            dst_ref=xs.at[l, h, r],
            send_sem=xsend.at[l, h, k - 1],
            recv_sem=xrecv.at[l, h, k - 1],
            device_id={"prow": lax.rem(r + k, rows)},
            device_id_type=MESH,
        )

    def p_copy(l, h, k):
        return pltpu.make_async_remote_copy(
            src_ref=part_out.at[l - 1, h, k - 1],
            dst_ref=part_in.at[l - 1, h, k - 1],
            send_sem=psend.at[l - 1, h, k - 1],
            recv_sem=precv.at[l - 1, h, k - 1],
            device_id={"pcol": lax.rem(c + k, cols)},
            device_id_type=MESH,
        )

    def merge(l):
        load(l).wait()
        piece = 32

        def source(s, carry):
            same = {}
            for m in range(nbr):
                for n in range(m + 1, nbr):
                    first = slots[l, s, m]
                    later = slots[l, s, n]
                    same[m, n] = jnp.where(first == later, 1.0, 0.0).astype(F32)
            for i in range(size // piece):
                at = pl.ds(i * piece, piece)
                vals = [raw[l, s * nbr + m, at, :].astype(F32) for m in range(nbr)]
                for m in range(nbr):
                    total = vals[m]
                    for n in range(m + 1, nbr):
                        total = total + same[m, n] * vals[n]
                    merged[l, s * nbr + m, at, :] = total.astype(BF16)
            return carry

        lax.fori_loop(0, rows, source, 0)
        merged[l, per] = jnp.zeros((size, size), BF16)

    def lhs_of(l, h):
        return jnp.concatenate([xs[l, h, s] for s in range(rows)], axis=1)

    def factor(target, owner, l):
        base = ((target * cols + owner) * steps + l) * rows
        return jnp.concatenate([merged[l, table[base + s]] for s in range(rows)], axis=1)

    def deferred(target):
        if target < 2:
            return

        def column(k, carry):
            owner = lax.rem(c + k, cols)
            total = None
            for l in range(target - 1):
                lhs = jnp.concatenate([lhs_of(l, h) for h in range(CHUNKS)], axis=0)
                term = dot_nt(lhs, factor(target, owner, l))
                total = term if total is None else total + term
            acc[k] = total
            return carry

        lax.fori_loop(0, cols, column, 0)

    def partials(l, h):
        lhs = lhs_of(l - 1, h)
        at = pl.ds(h * half, half)
        for k in list(range(1, cols)) + [0]:
            value = dot_nt(lhs, factor(l, lax.rem(c + k, cols), l - 1))
            if l >= 2:
                value = value + acc[k, at, :]
            if k:
                part_out[l - 1, h, k - 1] = value.astype(BF16)
                p_copy(l, h, k).start()
            else:
                own[h] = value

    def solve(l, h):
        at = pl.ds(h * half, half)
        residual = rst[l, at, :]
        if l:
            update = own[h]
            for k in range(1, cols):
                p_copy(l, h, k).wait_recv()
                update = update + part_in[l - 1, h, k - 1].astype(F32)
            residual = residual - update
        solved = dot_nt(residual.astype(BF16), inv[l]).astype(BF16)
        if l < steps:
            xs[l, h, r] = solved
            for k in range(1, rows):
                x_copy(l, h, k).start()
        return solved

    def finish(l, pieces):
        whole = jnp.concatenate([p.astype(F32) for p in pieces], axis=0)
        out[l] = whole.T.astype(BF16)

    rst[0] = rs[0].astype(F32).T
    pl.semaphore_wait(barrier, cols + rows - 2)

    pieces = [solve(0, h) for h in range(CHUNKS)]
    for l in range(1, levels):
        rst[l] = rs[l].astype(F32).T
    merge(0)
    finish(0, pieces)
    for l in range(1, levels):
        for h in range(CHUNKS):
            for k in range(1, rows):
                x_copy(l - 1, h, k).wait_recv()
            partials(l, h)
        if l < steps:
            merge(l)
            deferred(l + 1)
        pieces = [solve(l, h) for h in range(CHUNKS)]
        finish(l, pieces)

    for l in range(steps):
        for h in range(CHUNKS):
            for k in range(1, rows):
                x_copy(l, h, k).wait_send()
            for k in range(1, cols):
                p_copy(l + 1, h, k).wait_send()


def body(rows, cols, right_sides, inverses, blocks, targets):
    levels, size, rhs = right_sides.shape[0], right_sides.shape[4], right_sides.shape[5]
    steps = levels - 1
    nbr = targets.shape[-1]
    per = rows * nbr
    half = rhs // CHUNKS
    slots = targets.reshape(steps, rows, nbr) // rows
    place = jnp.arange(per, dtype=jnp.int32).reshape(rows, nbr)
    every = jnp.arange(levels * cols, dtype=jnp.int32)[:, None, None, None]
    table = jnp.min(jnp.where(slots[None] == every, place, per), axis=-1).reshape(-1)
    vmem = pl.BlockSpec(memory_space=pltpu.VMEM)
    smem = pl.BlockSpec(memory_space=pltpu.SMEM)
    solved = pl.pallas_call(
        functools.partial(kernel, (levels, rows, cols, nbr, size, rhs)),
        out_shape=jax.ShapeDtypeStruct((levels, size, rhs), BF16),
        in_specs=[smem, smem, vmem, vmem, pl.BlockSpec(memory_space=pl.ANY)],
        out_specs=vmem,
        scratch_shapes=[
            pltpu.VMEM((steps, per, size, size), BF16),
            pltpu.VMEM((steps, per + 1, size, size), BF16),
            pltpu.VMEM((steps, CHUNKS, rows, half, size), BF16),
            pltpu.VMEM((steps, CHUNKS, cols - 1, half, size), BF16),
            pltpu.VMEM((steps, CHUNKS, cols - 1, half, size), BF16),
            pltpu.VMEM((cols, rhs, size), F32),
            pltpu.VMEM((CHUNKS, half, size), F32),
            pltpu.VMEM((levels, rhs, size), F32),
            pltpu.SemaphoreType.DMA((steps,)),
            pltpu.SemaphoreType.DMA((steps, CHUNKS, rows - 1)),
            pltpu.SemaphoreType.DMA((steps, CHUNKS, rows - 1)),
            pltpu.SemaphoreType.DMA((steps, CHUNKS, cols - 1)),
            pltpu.SemaphoreType.DMA((steps, CHUNKS, cols - 1)),
        ],
        compiler_params=pltpu.CompilerParams(
            collective_id=0, has_side_effects=True, vmem_limit_bytes=52 * 1024 * 1024
        ),
    )(
        table,
        slots,
        right_sides.reshape(levels, size, rhs),
        inverses.reshape(levels, size, size),
        blocks.reshape(steps, per, size, size),
    )
    return solved.reshape(right_sides.shape)


def solution(mesh):
    in_specs = (
        P(None, None, "pcol", "prow", None, None),
        P(None, None, "pcol", "prow", None, None),
        P(None, None, "pcol", None, "prow", None, None, None),
        P(None, None, "pcol", None, "prow", None),
    )
    out_specs = P(None, None, "pcol", "prow", None, None)
    inner = functools.partial(body, mesh.shape["prow"], mesh.shape["pcol"])
    return jax.shard_map(inner, mesh=mesh, in_specs=in_specs, out_specs=out_specs, check_vma=False)
```

profile of v0, /device:TPU:0, one launch (start us, length us, event | category | flops | bytes accessed | tf_op | source)
XLA Modules:
  0.0 78.9 jit_solution(7014584288314123069)
XLA Ops:
  0.0 0.7 add_select_fusion.slots
  0.7 0.2 select_reduce_fusion
  0.9 0.2 copy.7
  1.1 0.1 reshape.57.table
  1.2 0.0 copy-start
  1.2 0.9 %copy-done = bf16[8,1,1,1,128,128]{5,4,3,2,1,0:T(8,128)(2,1)S(1)} copy-done((bf16[8,1,1,1,128,128]{5,4,3,2,1,0:T(8,128)(2,1)S(1)}, bf16[8,1,1,1,128,128]{5,4,3,2,1,0:T(8,128)(2,1)}, u32[]{:S(2)}) %copy-start) | copy-done | bytes 262168
  2.2 0.0 copy-start.1
  2.2 0.9 %copy-done.1 = bf16[8,1,1,1,128,128]{5,4,3,2,1,0:T(8,128)(2,1)S(1)} copy-done((bf16[8,1,1,1,128,128]{5,4,3,2,1,0:T(8,128)(2,1)S(1)}, bf16[8,1,1,1,128,128]{5,4,3,2,1,0:T(8,128)(2,1)}, u32[]{:S(2)}) %copy-start.1) | copy-done | bytes 262168
  3.1 75.0 %shard_map.46 = bf16[8,128,128]{2,1,0:T(8,128)(2,1)S(1)} custom-call(s32[1792]{0:T(1024)S(1)} %reshape.57.table, s32[7,4,8]{2,1,0:T(4,128)S(1)} %add_select_fusion.slots, bf16[8,128,128]{2,1,0:T(8,128)(2,1)S(1)} %bitcast.8, bf16[8,128,128]{2,1,0:T(8,128)(2,1)S(1)} %bitcast.9, bf16[7,32,128,128]{3,2,1,0:T(8,128)(2,1)} %bitcast.10), custom_call_target="tpu_custom_call" | custom-call | tf_op jit(solution)/shard_map/pallas_call | solution.py:204
  78.2 0.7 copy.10
  (1 shorter events, 0.0 us)
Async XLA Ops:
  1.2 1.0 %copy-start = (bf16[8,1,1,1,128,128]{5,4,3,2,1,0:T(8,128)(2,1)S(1)}, bf16[8,1,1,1,128,128]{5,4,3,2,1,0:T(8,128)(2,1)}, u32[]{:S(2)}) copy-start(bf16[8,1,1,1,128,128]{5,4,3,2,1,0:T(8,128)(2,1)} %param.4) | copy-start | bytes 786436
  2.2 0.9 %copy-start.1 = (bf16[8,1,1,1,128,128]{5,4,3,2,1,0:T(8,128)(2,1)S(1)}, bf16[8,1,1,1,128,128]{5,4,3,2,1,0:T(8,128)(2,1)}, u32[]{:S(2)}) copy-start(bf16[8,1,1,1,128,128]{5,4,3,2,1,0:T(8,128)(2,1)} %param.5) | copy-start | bytes 786436
where the time goes:
time: 79.1 us; the launch traced here: 78.9 us
  Pallas kernels  75 us (95%)
  local copies, waits for them, and re-layouts  2.91 us (4%)
  other arithmetic  0.9 us (1%)
    pallas_call x1, Pallas kernels, body(): pl.pallas_call(functools.partial(kernel, (levels, rows, cols, nbr, size,...  75 us
    unnamed x5, local copies, waits for them, and re-layouts  2.6 us

commit v1 on v0

--- a/solution.py
+++ b/solution.py
@@ -8,13 +8,23 @@
 from jax.sharding import PartitionSpec as P
 
 MESH = pl.DeviceIdType.MESH
-CHUNKS = 1
+CHUNKS = 2
+GROUP = 4
 F32 = jnp.float32
 BF16 = jnp.bfloat16
 
 
 def dot_nt(a, b):
     return lax.dot_general(a, b, (((1,), (1,)), ((), ())), preferred_element_type=F32)
+
+
+def flip(a, k, n):
+    total = 0
+    w = 1
+    while w < n:
+        total = total + lax.rem(a // w + k // w, 2) * w
+        w *= 2
+    return total
 
 
 def kernel(
@@ -46,6 +56,11 @@
     r = lax.axis_index("prow")
     c = lax.axis_index("pcol")
 
+    col_order = sorted(range(1, cols), key=lambda k: (-bin(k // 2).count("1"), k % 2, k))
+    row_order = list(range(rows - 1, 0, -1))
+    col_peer = [flip(c, k, cols) for k in range(cols)]
+    row_peer = [flip(r, k, rows) for k in range(rows)]
+
     def load(l):
         return pltpu.make_async_copy(blocks.at[l], raw.at[l], load_sem.at[l])
 
@@ -55,11 +70,11 @@
     barrier = pltpu.get_barrier_semaphore()
     for k in range(1, cols):
         pl.semaphore_signal(
-            barrier, inc=1, device_id={"pcol": lax.rem(c + k, cols)}, device_id_type=MESH
+            barrier, inc=1, device_id={"pcol": col_peer[k]}, device_id_type=MESH
         )
     for k in range(1, rows):
         pl.semaphore_signal(
-            barrier, inc=1, device_id={"prow": lax.rem(r + k, rows)}, device_id_type=MESH
+            barrier, inc=1, device_id={"prow": row_peer[k]}, device_id_type=MESH
         )
 
     def x_copy(l, h, k):
@@ -68,7 +83,7 @@
             dst_ref=xs.at[l, h, r],
             send_sem=xsend.at[l, h, k - 1],
             recv_sem=xrecv.at[l, h, k - 1],
-            device_id={"prow": lax.rem(r + k, rows)},
+            device_id={"prow": row_peer[k]},
             device_id_type=MESH,
         )
 
@@ -78,7 +93,7 @@
             dst_ref=part_in.at[l - 1, h, k - 1],
             send_sem=psend.at[l - 1, h, k - 1],
             recv_sem=precv.at[l - 1, h, k - 1],
-            device_id={"pcol": lax.rem(c + k, cols)},
+            device_id={"pcol": col_peer[k]},
             device_id_type=MESH,
         )
 
@@ -113,34 +128,34 @@
         base = ((target * cols + owner) * steps + l) * rows
         return jnp.concatenate([merged[l, table[base + s]] for s in range(rows)], axis=1)
 
-    def deferred(target):
-        if target < 2:
-            return
-
-        def column(k, carry):
-            owner = lax.rem(c + k, cols)
-            total = None
-            for l in range(target - 1):
-                lhs = jnp.concatenate([lhs_of(l, h) for h in range(CHUNKS)], axis=0)
-                term = dot_nt(lhs, factor(target, owner, l))
-                total = term if total is None else total + term
-            acc[k] = total
+    def deferred(target, first, last):
+        def columns(group, carry):
+            for i in range(GROUP):
+                k = group * GROUP + i
+                owner = flip(c, k, cols)
+                total = acc[target % 2, k] if first else None
+                for l in range(first, last):
+                    lhs = jnp.concatenate([lhs_of(l, h) for h in range(CHUNKS)], axis=0)
+                    term = dot_nt(lhs, factor(target, owner, l))
+                    total = term if total is None else total + term
+                acc[target % 2, k] = total
             return carry
 
-        lax.fori_loop(0, cols, column, 0)
+        lax.fori_loop(0, cols // GROUP, columns, 0)
 
     def partials(l, h):
         lhs = lhs_of(l - 1, h)
         at = pl.ds(h * half, half)
-        for k in list(range(1, cols)) + [0]:
-            value = dot_nt(lhs, factor(l, lax.rem(c + k, cols), l - 1))
+        for k in col_order + [0]:
+            value = dot_nt(lhs, factor(l, col_peer[k], l - 1))
             if l >= 2:
-                value = value + acc[k, at, :]
+                value = value + acc[l % 2, k, at, :]
             if k:
                 part_out[l - 1, h, k - 1] = value.astype(BF16)
-                p_copy(l, h, k).start()
             else:
                 own[h] = value
+        for k in col_order:
+            p_copy(l, h, k).start()
 
     def solve(l, h):
         at = pl.ds(h * half, half)
@@ -154,7 +169,7 @@
         solved = dot_nt(residual.astype(BF16), inv[l]).astype(BF16)
         if l < steps:
             xs[l, h, r] = solved
-            for k in range(1, rows):
+            for k in row_order:
                 x_copy(l, h, k).start()
         return solved
 
@@ -177,9 +192,11 @@
             partials(l, h)
         if l < steps:
             merge(l)
-            deferred(l + 1)
+            deferred(l + 1, l - 1, l)
         pieces = [solve(l, h) for h in range(CHUNKS)]
         finish(l, pieces)
+        if l + 2 < levels:
+            deferred(l + 2, 0, l)
 
     for l in range(steps):
         for h in range(CHUNKS):
@@ -212,7 +229,7 @@
             pltpu.VMEM((steps, CHUNKS, rows, half, size), BF16),
             pltpu.VMEM((steps, CHUNKS, cols - 1, half, size), BF16),
             pltpu.VMEM((steps, CHUNKS, cols - 1, half, size), BF16),
-            pltpu.VMEM((cols, rhs, size), F32),
+            pltpu.VMEM((2, cols, rhs, size), F32),
             pltpu.VMEM((CHUNKS, half, size), F32),
             pltpu.VMEM((levels, rhs, size), F32),
             pltpu.SemaphoreType.DMA((steps,)),

time: 79.1 us -> 71.9 us (0.909)
  Pallas kernels: 75 us -> 67.8 us
    pallas_call x1, Pallas kernels: 75 us -> 67.8 us  [body(): pl.pallas_call(functools.partial(kernel, (levels, rows, cols, nbr, size,...]
where the time goes in v1:
time: 71.9 us; the launch traced here: 71.6 us
  Pallas kernels  67.8 us (94%)
  local copies, waits for them, and re-layouts  2.91 us (4%)
  other arithmetic  0.9 us (1%)
    pallas_call x1, Pallas kernels, body(): pl.pallas_call(functools.partial(kernel, (levels, rows, cols, nbr, size,...  67.8 us
    unnamed x5, local copies, waits for them, and re-layouts  2.6 us

profile of v1, /device:TPU:0, one launch (start us, length us, event | category | flops | bytes accessed | tf_op | source)
XLA Modules:
  0.0 71.6 jit_solution(17783003421327624032)
XLA Ops:
  0.0 0.7 %add_select_fusion.slots = s32[7,4,8]{2,1,0:T(4,128)S(1)} fusion(s32[7,4,8]{2,1,0:T(4,128)} %bitcast.11), kind=kLoop, calls=%fused_computation.2 | loop fusion | flops 3360 | bytes 1792 | tf_op jit(solution)/shard_map/jit(floor_divide)/jit(_where)/select_n | solution.py:215
  0.7 0.2 select_reduce_fusion
  0.9 0.2 copy.7
  1.1 0.1 reshape.57.table
  1.2 0.0 copy-start
  1.2 0.9 %copy-done = bf16[8,1,1,1,128,128]{5,4,3,2,1,0:T(8,128)(2,1)S(1)} copy-done((bf16[8,1,1,1,128,128]{5,4,3,2,1,0:T(8,128)(2,1)S(1)}, bf16[8,1,1,1,128,128]{5,4,3,2,1,0:T(8,128)(2,1)}, u32[]{:S(2)}) %copy-start) | copy-done | bytes 262168
  2.2 0.0 copy-start.1
  2.2 0.9 %copy-done.1 = bf16[8,1,1,1,128,128]{5,4,3,2,1,0:T(8,128)(2,1)S(1)} copy-done((bf16[8,1,1,1,128,128]{5,4,3,2,1,0:T(8,128)(2,1)S(1)}, bf16[8,1,1,1,128,128]{5,4,3,2,1,0:T(8,128)(2,1)}, u32[]{:S(2)}) %copy-start.1) | copy-done | bytes 262168
  3.1 67.8 %shard_map.46 = bf16[8,128,128]{2,1,0:T(8,128)(2,1)S(1)} custom-call(s32[1792]{0:T(1024)S(1)} %reshape.57.table, s32[7,4,8]{2,1,0:T(4,128)S(1)} %add_select_fusion.slots, bf16[8,128,128]{2,1,0:T(8,128)(2,1)S(1)} %bitcast.8, bf16[8,128,128]{2,1,0:T(8,128)(2,1)S(1)} %bitcast.9, bf16[7,32,128,128]{3,2,1,0:T(8,128)(2,1)} %bitcast.10), custom_call_target="tpu_custom_call" | custom-call | tf_op jit(solution)/shard_map/pallas_call | solution.py:221
  70.9 0.7 copy.10
  (1 shorter events, 0.0 us)
Async XLA Ops:
  1.2 1.0 %copy-start = (bf16[8,1,1,1,128,128]{5,4,3,2,1,0:T(8,128)(2,1)S(1)}, bf16[8,1,1,1,128,128]{5,4,3,2,1,0:T(8,128)(2,1)}, u32[]{:S(2)}) copy-start(bf16[8,1,1,1,128,128]{5,4,3,2,1,0:T(8,128)(2,1)} %param.4) | copy-start | bytes 786436
  2.2 0.9 %copy-start.1 = (bf16[8,1,1,1,128,128]{5,4,3,2,1,0:T(8,128)(2,1)S(1)}, bf16[8,1,1,1,128,128]{5,4,3,2,1,0:T(8,128)(2,1)}, u32[]{:S(2)}) copy-start(bf16[8,1,1,1,128,128]{5,4,3,2,1,0:T(8,128)(2,1)} %param.5) | copy-start | bytes 786436

commit v2 on v1

--- a/solution.py
+++ b/solution.py
@@ -8,7 +8,7 @@
 from jax.sharding import PartitionSpec as P
 
 MESH = pl.DeviceIdType.MESH
-CHUNKS = 2
+CHUNKS = 4
 GROUP = 4
 F32 = jnp.float32
 BF16 = jnp.bfloat16
@@ -81,8 +81,8 @@
         return pltpu.make_async_remote_copy(
             src_ref=xs.at[l, h, r],
             dst_ref=xs.at[l, h, r],
-            send_sem=xsend.at[l, h, k - 1],
-            recv_sem=xrecv.at[l, h, k - 1],
+            send_sem=xsend.at[l],
+            recv_sem=xrecv.at[l, h],
             device_id={"prow": row_peer[k]},
             device_id_type=MESH,
         )
@@ -91,11 +91,14 @@
         return pltpu.make_async_remote_copy(
             src_ref=part_out.at[l - 1, h, k - 1],
             dst_ref=part_in.at[l - 1, h, k - 1],
-            send_sem=psend.at[l - 1, h, k - 1],
-            recv_sem=precv.at[l - 1, h, k - 1],
+            send_sem=psend.at[l - 1],
+            recv_sem=precv.at[l - 1, h],
             device_id={"pcol": col_peer[k]},
             device_id_type=MESH,
         )
+
+    def waiting(ref, sem):
+        pltpu.make_async_copy(ref, ref, sem).wait()
 
     def merge(l):
         load(l).wait()
@@ -162,8 +165,8 @@
         residual = rst[l, at, :]
         if l:
             update = own[h]
+            waiting(part_in.at[l - 1, h], precv.at[l - 1, h])
             for k in range(1, cols):
-                p_copy(l, h, k).wait_recv()
                 update = update + part_in[l - 1, h, k - 1].astype(F32)
             residual = residual - update
         solved = dot_nt(residual.astype(BF16), inv[l]).astype(BF16)
@@ -187,8 +190,7 @@
     finish(0, pieces)
     for l in range(1, levels):
         for h in range(CHUNKS):
-            for k in range(1, rows):
-                x_copy(l - 1, h, k).wait_recv()
+            waiting(xs.at[l - 1, h, pl.ds(0, rows - 1)], xrecv.at[l - 1, h])
             partials(l, h)
         if l < steps:
             merge(l)
@@ -199,11 +201,8 @@
             deferred(l + 2, 0, l)
 
     for l in range(steps):
-        for h in range(CHUNKS):
-            for k in range(1, rows):
-                x_copy(l, h, k).wait_send()
-            for k in range(1, cols):
-                p_copy(l + 1, h, k).wait_send()
+        waiting(xs.at[l, :, pl.ds(0, rows - 1)], xsend.at[l])
+        waiting(part_out.at[l], psend.at[l])
 
 
 def body(rows, cols, right_sides, inverses, blocks, targets):
@@ -233,10 +232,10 @@
             pltpu.VMEM((CHUNKS, half, size), F32),
             pltpu.VMEM((levels, rhs, size), F32),
             pltpu.SemaphoreType.DMA((steps,)),
-            pltpu.SemaphoreType.DMA((steps, CHUNKS, rows - 1)),
-            pltpu.SemaphoreType.DMA((steps, CHUNKS, rows - 1)),
-            pltpu.SemaphoreType.DMA((steps, CHUNKS, cols - 1)),
-            pltpu.SemaphoreType.DMA((steps, CHUNKS, cols - 1)),
+            pltpu.SemaphoreType.DMA((steps,)),
+            pltpu.SemaphoreType.DMA((steps, CHUNKS)),
+            pltpu.SemaphoreType.DMA((steps,)),
+            pltpu.SemaphoreType.DMA((steps, CHUNKS)),
         ],
         compiler_params=pltpu.CompilerParams(
             collective_id=0, has_side_effects=True, vmem_limit_bytes=52 * 1024 * 1024

time: 71.9 us -> 65.5 us (0.911)
  Pallas kernels: 67.8 us -> 61.4 us
    pallas_call x1, Pallas kernels: 67.8 us -> 61.4 us  [body(): pl.pallas_call(functools.partial(kernel, (levels, rows, cols, nbr, size,...]
where the time goes in v2:
time: 65.5 us; the launch traced here: 65.3 us
  Pallas kernels  61.4 us (94%)
  local copies, waits for them, and re-layouts  2.91 us (4%)
  other arithmetic  0.9 us (1%)
    pallas_call x1, Pallas kernels, body(): pl.pallas_call(functools.partial(kernel, (levels, rows, cols, nbr, size,...  61.4 us
    unnamed x5, local copies, waits for them, and re-layouts  2.6 us

profile of v2, /device:TPU:0, one launch (start us, length us, event | category | flops | bytes accessed | tf_op | source)
XLA Modules:
  0.0 65.3 jit_solution(8640340217553904481)
XLA Ops:
  0.0 0.7 %add_select_fusion.slots = s32[7,4,8]{2,1,0:T(4,128)S(1)} fusion(s32[7,4,8]{2,1,0:T(4,128)} %bitcast.11), kind=kLoop, calls=%fused_computation.2 | loop fusion | flops 3360 | bytes 1792 | tf_op jit(solution)/shard_map/jit(floor_divide)/jit(_where)/select_n | solution.py:214
  0.7 0.2 select_reduce_fusion
  0.9 0.2 copy.7
  1.1 0.1 reshape.57.table
  1.2 0.0 copy-start
  1.2 0.9 %copy-done = bf16[8,1,1,1,128,128]{5,4,3,2,1,0:T(8,128)(2,1)S(1)} copy-done((bf16[8,1,1,1,128,128]{5,4,3,2,1,0:T(8,128)(2,1)S(1)}, bf16[8,1,1,1,128,128]{5,4,3,2,1,0:T(8,128)(2,1)}, u32[]{:S(2)}) %copy-start) | copy-done | bytes 262168
  2.2 0.0 copy-start.1
  2.2 0.9 %copy-done.1 = bf16[8,1,1,1,128,128]{5,4,3,2,1,0:T(8,128)(2,1)S(1)} copy-done((bf16[8,1,1,1,128,128]{5,4,3,2,1,0:T(8,128)(2,1)S(1)}, bf16[8,1,1,1,128,128]{5,4,3,2,1,0:T(8,128)(2,1)}, u32[]{:S(2)}) %copy-start.1) | copy-done | bytes 262168
  3.1 61.4 %shard_map.46 = bf16[8,128,128]{2,1,0:T(8,128)(2,1)S(1)} custom-call(s32[1792]{0:T(1024)S(1)} %reshape.57.table, s32[7,4,8]{2,1,0:T(4,128)S(1)} %add_select_fusion.slots, bf16[8,128,128]{2,1,0:T(8,128)(2,1)S(1)} %bitcast.8, bf16[8,128,128]{2,1,0:T(8,128)(2,1)S(1)} %bitcast.9, bf16[7,32,128,128]{3,2,1,0:T(8,128)(2,1)} %bitcast.10), custom_call_target="tpu_custom_call" | custom-call | tf_op jit(solution)/shard_map/pallas_call | solution.py:220
  64.5 0.7 %copy.10 = bf16[8,1,1,1,128,128]{5,4,3,2,1,0:T(8,128)(2,1)} copy(bf16[8,1,1,1,128,128]{5,4,3,2,1,0:T(8,128)(2,1)S(1)} %bitcast.7) | data formatting | bytes 524288
  (1 shorter events, 0.0 us)
Async XLA Ops:
  1.2 1.0 %copy-start = (bf16[8,1,1,1,128,128]{5,4,3,2,1,0:T(8,128)(2,1)S(1)}, bf16[8,1,1,1,128,128]{5,4,3,2,1,0:T(8,128)(2,1)}, u32[]{:S(2)}) copy-start(bf16[8,1,1,1,128,128]{5,4,3,2,1,0:T(8,128)(2,1)} %param.4) | copy-start | bytes 786436
  2.2 0.9 %copy-start.1 = (bf16[8,1,1,1,128,128]{5,4,3,2,1,0:T(8,128)(2,1)S(1)}, bf16[8,1,1,1,128,128]{5,4,3,2,1,0:T(8,128)(2,1)}, u32[]{:S(2)}) copy-start(bf16[8,1,1,1,128,128]{5,4,3,2,1,0:T(8,128)(2,1)} %param.5) | copy-start | bytes 786436

commit v3 on v2

--- a/solution.py
+++ b/solution.py
@@ -31,8 +31,8 @@
     dims,
     table,
     slots,
-    rs,
-    inv,
+    rs_hbm,
+    inv_hbm,
     blocks,
     out,
     raw,
@@ -43,6 +43,9 @@
     acc,
     own,
     rst,
+    rs,
+    inv,
+    in_sem,
     load_sem,
     xsend,
     xrecv,
@@ -64,6 +67,13 @@
     def load(l):
         return pltpu.make_async_copy(blocks.at[l], raw.at[l], load_sem.at[l])
 
+    inputs = []
+    for at in (pl.ds(0, 1), pl.ds(1, steps)):
+        for src, dst in ((rs_hbm, rs), (inv_hbm, inv)):
+            sem = in_sem.at[len(inputs)]
+            inputs.append(pltpu.make_async_copy(src.at[at], dst.at[at], sem))
+    for copy in inputs:
+        copy.start()
     for l in range(steps):
         load(l).start()
 
@@ -128,8 +138,8 @@
         return jnp.concatenate([xs[l, h, s] for s in range(rows)], axis=1)
 
     def factor(target, owner, l):
-        base = ((target * cols + owner) * steps + l) * rows
-        return jnp.concatenate([merged[l, table[base + s]] for s in range(rows)], axis=1)
+        at = target * cols + owner
+        return jnp.concatenate([merged[l, table[l, s, at]] for s in range(rows)], axis=1)
 
     def deferred(target, first, last):
         def columns(group, carry):
@@ -169,21 +179,27 @@
             for k in range(1, cols):
                 update = update + part_in[l - 1, h, k - 1].astype(F32)
             residual = residual - update
-        solved = dot_nt(residual.astype(BF16), inv[l]).astype(BF16)
-        if l < steps:
-            xs[l, h, r] = solved
-            for k in row_order:
-                x_copy(l, h, k).start()
+        residual = residual.astype(BF16)
+        if l == steps:
+            return residual
+        solved = dot_nt(residual, inv[l]).astype(BF16)
+        xs[l, h, r] = solved
+        for k in row_order:
+            x_copy(l, h, k).start()
         return solved
 
     def finish(l, pieces):
         whole = jnp.concatenate([p.astype(F32) for p in pieces], axis=0)
         out[l] = whole.T.astype(BF16)
 
+    for copy in inputs[:2]:
+        copy.wait()
     rst[0] = rs[0].astype(F32).T
     pl.semaphore_wait(barrier, cols + rows - 2)
 
     pieces = [solve(0, h) for h in range(CHUNKS)]
+    for copy in inputs[2:]:
+        copy.wait()
     for l in range(1, levels):
         rst[l] = rs[l].astype(F32).T
     merge(0)
@@ -196,7 +212,10 @@
             merge(l)
             deferred(l + 1, l - 1, l)
         pieces = [solve(l, h) for h in range(CHUNKS)]
-        finish(l, pieces)
+        if l < steps:
+            finish(l, pieces)
+        else:
+            out[l] = dot_nt(inv[l], jnp.concatenate(pieces, axis=0)).astype(BF16)
         if l + 2 < levels:
             deferred(l + 2, 0, l)
 
@@ -213,14 +232,15 @@
     half = rhs // CHUNKS
     slots = targets.reshape(steps, rows, nbr) // rows
     place = jnp.arange(per, dtype=jnp.int32).reshape(rows, nbr)
-    every = jnp.arange(levels * cols, dtype=jnp.int32)[:, None, None, None]
-    table = jnp.min(jnp.where(slots[None] == every, place, per), axis=-1).reshape(-1)
+    every = jnp.arange(levels * cols, dtype=jnp.int32)[None, None, :, None]
+    found = slots[:, :, None] == every
+    table = jnp.min(jnp.where(found, place[None, :, None], per), axis=-1)
     vmem = pl.BlockSpec(memory_space=pltpu.VMEM)
     smem = pl.BlockSpec(memory_space=pltpu.SMEM)
     solved = pl.pallas_call(
         functools.partial(kernel, (levels, rows, cols, nbr, size, rhs)),
         out_shape=jax.ShapeDtypeStruct((levels, size, rhs), BF16),
-        in_specs=[smem, smem, vmem, vmem, pl.BlockSpec(memory_space=pl.ANY)],
+        in_specs=[smem, smem] + [pl.BlockSpec(memory_space=pltpu.HBM)] * 3,
         out_specs=vmem,
         scratch_shapes=[
             pltpu.VMEM((steps, per, size, size), BF16),
@@ -231,6 +251,9 @@
             pltpu.VMEM((2, cols, rhs, size), F32),
             pltpu.VMEM((CHUNKS, half, size), F32),
             pltpu.VMEM((levels, rhs, size), F32),
+            pltpu.VMEM((levels, size, rhs), BF16),
+            pltpu.VMEM((levels, size, size), BF16),
+            pltpu.SemaphoreType.DMA((4,)),
             pltpu.SemaphoreType.DMA((steps,)),
             pltpu.SemaphoreType.DMA((steps,)),
             pltpu.SemaphoreType.DMA((steps, CHUNKS)),
@@ -238,7 +261,7 @@
             pltpu.SemaphoreType.DMA((steps, CHUNKS)),
         ],
         compiler_params=pltpu.CompilerParams(
-            collective_id=0, has_side_effects=True, vmem_limit_bytes=52 * 1024 * 1024
+            collective_id=0, has_side_effects=True, vmem_limit_bytes=54784 * 1024
         ),
     )(
         table,

time: 65.5 us -> 63.5 us (0.969)
  local copies, waits for them, and re-layouts: 2.91 us -> 0.71 us
    unnamed x5 -> x1, local copies, waits for them, and re-layouts: 2.6 us -> 0.71 us
where the time goes in v3:
time: 63.5 us; the launch traced here: 63.3 us
  Pallas kernels  61.6 us (97%)
  other arithmetic  0.9 us (1%)
  local copies, waits for them, and re-layouts  0.71 us (1%)
    pallas_call x1, Pallas kernels, body(): pl.pallas_call(functools.partial(kernel, (levels, rows, cols, nbr, size,...  61.6 us

profile of v3, /device:TPU:0, one launch (start us, length us, event | category | flops | bytes accessed | tf_op | source)
XLA Modules:
  0.0 63.3 jit_solution(14931365163502587838)
XLA Ops:
  0.0 0.7 %add_select_fusion.slots = s32[7,4,8]{2,1,0:T(4,128)S(1)} fusion(s32[7,4,8]{2,1,0:T(4,128)} %bitcast.11), kind=kLoop, calls=%fused_computation.2 | loop fusion | flops 3360 | bytes 1792 | tf_op jit(solution)/shard_map/jit(floor_divide)/jit(_where)/select_n | solution.py:233
  0.7 0.2 select_reduce_fusion.table
  0.9 61.6 %shard_map.46 = bf16[8,128,128]{2,1,0:T(8,128)(2,1)S(1)} custom-call(s32[7,4,64]{2,1,0:T(4,128)S(1)} %select_reduce_fusion.table, s32[7,4,8]{2,1,0:T(4,128)S(1)} %add_select_fusion.slots, bf16[8,128,128]{2,1,0:T(8,128)(2,1)} %bitcast.9, bf16[8,128,128]{2,1,0:T(8,128)(2,1)} %bitcast.10, bf16[7,32,128,128]{3,2,1,0:T(8,128)(2,1)} %bitcast.8), custom_call_target="tpu_custom_call" | custom-call | tf_op jit(solution)/shard_map/pallas_call | solution.py:240
  62.5 0.7 %copy.8 = bf16[8,1,1,1,128,128]{5,4,3,2,1,0:T(8,128)(2,1)} copy(bf16[8,1,1,1,128,128]{5,4,3,2,1,0:T(8,128)(2,1)S(1)} %bitcast.7) | data formatting | bytes 524288
  (1 shorter events, 0.0 us)

commit v4 on v3

--- a/solution.py
+++ b/solution.py
@@ -29,8 +29,7 @@
 
 def kernel(
     dims,
-    table,
-    slots,
+    numbers,
     rs_hbm,
     inv_hbm,
     blocks,
@@ -45,6 +44,9 @@
     rst,
     rs,
     inv,
+    found,
+    table,
+    slots,
     in_sem,
     load_sem,
     xsend,
@@ -74,6 +76,8 @@
             inputs.append(pltpu.make_async_copy(src.at[at], dst.at[at], sem))
     for copy in inputs:
         copy.start()
+    listing = pltpu.make_async_copy(numbers, slots, in_sem.at[4])
+    listing.start()
     for l in range(steps):
         load(l).start()
 
@@ -110,6 +114,23 @@
     def waiting(ref, sem):
         pltpu.make_async_copy(ref, ref, sem).wait()
 
+    def index():
+        listing.wait()
+        wanted = lax.broadcasted_iota(jnp.int32, (1, found.shape[1]), 1) * rows + r
+
+        def line(i, carry):
+            base = lax.rem(i, rows) * nbr
+            place = jnp.full(wanted.shape, per, jnp.int32)
+            for m in reversed(range(nbr)):
+                place = jnp.where(wanted == slots[i, 0, m], base + m, place)
+            found[pl.ds(i, 1), :] = place
+            return carry
+
+        lax.fori_loop(0, steps * rows, line, 0)
+        filed = pltpu.make_async_copy(found, table, in_sem.at[5])
+        filed.start()
+        return filed
+
     def merge(l):
         load(l).wait()
         piece = 32
@@ -118,8 +139,8 @@
             same = {}
             for m in range(nbr):
                 for n in range(m + 1, nbr):
-                    first = slots[l, s, m]
-                    later = slots[l, s, n]
+                    first = slots[l * rows + s, 0, m]
+                    later = slots[l * rows + s, 0, n]
                     same[m, n] = jnp.where(first == later, 1.0, 0.0).astype(F32)
             for i in range(size // piece):
                 at = pl.ds(i * piece, piece)
@@ -139,7 +160,7 @@
 
     def factor(target, owner, l):
         at = target * cols + owner
-        return jnp.concatenate([merged[l, table[l, s, at]] for s in range(rows)], axis=1)
+        return jnp.concatenate([merged[l, table[l * rows + s, at]] for s in range(rows)], axis=1)
 
     def deferred(target, first, last):
         def columns(group, carry):
@@ -170,22 +191,23 @@
         for k in col_order:
             p_copy(l, h, k).start()
 
+    def send(l, h, value):
+        xs[l, h, r] = value
+        for k in row_order:
+            x_copy(l, h, k).start()
+
     def solve(l, h):
         at = pl.ds(h * half, half)
-        residual = rst[l, at, :]
-        if l:
-            update = own[h]
-            waiting(part_in.at[l - 1, h], precv.at[l - 1, h])
-            for k in range(1, cols):
-                update = update + part_in[l - 1, h, k - 1].astype(F32)
-            residual = residual - update
+        waiting(part_in.at[l - 1, h], precv.at[l - 1, h])
+        update = own[h]
+        for k in range(1, cols):
+            update = update + part_in[l - 1, h, k - 1].astype(F32)
+        residual = rst[l, at, :] - update
         residual = residual.astype(BF16)
         if l == steps:
             return residual
         solved = dot_nt(residual, inv[l]).astype(BF16)
-        xs[l, h, r] = solved
-        for k in row_order:
-            x_copy(l, h, k).start()
+        send(l, h, solved)
         return solved
 
     def finish(l, pieces):
@@ -195,14 +217,19 @@
     for copy in inputs[:2]:
         copy.wait()
     rst[0] = rs[0].astype(F32).T
+    first = dot_nt(rst[0].astype(BF16), inv[0]).astype(BF16)
     pl.semaphore_wait(barrier, cols + rows - 2)
 
-    pieces = [solve(0, h) for h in range(CHUNKS)]
+    pieces = [first[h * half : (h + 1) * half] for h in range(CHUNKS)]
+    for h in range(CHUNKS):
+        send(0, h, pieces[h])
     for copy in inputs[2:]:
         copy.wait()
     for l in range(1, levels):
         rst[l] = rs[l].astype(F32).T
+    filed = index()
     merge(0)
+    filed.wait()
     finish(0, pieces)
     for l in range(1, levels):
         for h in range(CHUNKS):
@@ -230,17 +257,13 @@
     nbr = targets.shape[-1]
     per = rows * nbr
     half = rhs // CHUNKS
-    slots = targets.reshape(steps, rows, nbr) // rows
-    place = jnp.arange(per, dtype=jnp.int32).reshape(rows, nbr)
-    every = jnp.arange(levels * cols, dtype=jnp.int32)[None, None, :, None]
-    found = slots[:, :, None] == every
-    table = jnp.min(jnp.where(found, place[None, :, None], per), axis=-1)
+    lanes = -(-levels * cols // 128) * 128
+    lines = -(-steps * rows // 8) * 8
     vmem = pl.BlockSpec(memory_space=pltpu.VMEM)
-    smem = pl.BlockSpec(memory_space=pltpu.SMEM)
     solved = pl.pallas_call(
         functools.partial(kernel, (levels, rows, cols, nbr, size, rhs)),
         out_shape=jax.ShapeDtypeStruct((levels, size, rhs), BF16),
-        in_specs=[smem, smem] + [pl.BlockSpec(memory_space=pltpu.HBM)] * 3,
+        in_specs=[pl.BlockSpec(memory_space=pltpu.HBM)] * 4,
         out_specs=vmem,
         scratch_shapes=[
             pltpu.VMEM((steps, per, size, size), BF16),
@@ -253,7 +276,10 @@
             pltpu.VMEM((levels, rhs, size), F32),
             pltpu.VMEM((levels, size, rhs), BF16),
             pltpu.VMEM((levels, size, size), BF16),
-            pltpu.SemaphoreType.DMA((4,)),
+            pltpu.VMEM((lines, lanes), jnp.int32),
+            pltpu.SMEM((lines, lanes), jnp.int32),
+            pltpu.SMEM((steps * rows, 1, nbr), jnp.int32),
+            pltpu.SemaphoreType.DMA((6,)),
             pltpu.SemaphoreType.DMA((steps,)),
             pltpu.SemaphoreType.DMA((steps,)),
             pltpu.SemaphoreType.DMA((steps, CHUNKS)),
@@ -264,8 +290,7 @@
             collective_id=0, has_side_effects=True, vmem_limit_bytes=54784 * 1024
         ),
     )(
-        table,
-        slots,
+        targets.reshape(steps * rows, 1, nbr),
         right_sides.reshape(levels, size, rhs),
         inverses.reshape(levels, size, size),
         blocks.reshape(steps, per, size, size),

time: 63.5 us -> 62 us (0.976)
  Pallas kernels: 61.6 us -> 60.4 us
  other arithmetic: 0.9 us -> 0 us
  local copies, waits for them, and re-layouts: 0.71 us -> 1.42 us
    pallas_call x1, Pallas kernels: 61.6 us -> 60.4 us  [body(): pl.pallas_call(functools.partial(kernel, (levels, rows, cols, nbr, size,...]
    select_n x1 -> x0, other arithmetic: 0.73 us -> none  [body(): slots = targets.reshape(steps, rows, nbr) // rows]
    unnamed x1 -> x3, local copies, waits for them, and re-layouts: 0.71 us -> 1.42 us
where the time goes in v4:
time: 62 us; the launch traced here: 61.8 us
  Pallas kernels  60.4 us (97%)
  local copies, waits for them, and re-layouts  1.42 us (2%)
    pallas_call x1, Pallas kernels, body(): pl.pallas_call(functools.partial(kernel, (levels, rows, cols, nbr, size,...  60.4 us
    unnamed x3, local copies, waits for them, and re-layouts  1.42 us

profile of v4, /device:TPU:0, one launch (start us, length us, event | category | flops | bytes accessed | tf_op | source)
XLA Modules:
  0.0 61.8 jit_solution(17241256315788817339)
XLA Ops:
  0.0 0.0 copy-start
  0.0 0.7 %copy-done = s32[7,1,1,4,1,8]{5,4,3,2,1,0:T(1,128)S(1)} copy-done((s32[7,1,1,4,1,8]{5,4,3,2,1,0:T(1,128)S(1)}, s32[7,1,1,4,1,8]{5,4,3,2,1,0:T(1,128)}, u32[]{:S(2)}) %copy-start) | copy-done | bytes 920
  0.7 60.4 %shard_map.46 = bf16[8,128,128]{2,1,0:T(8,128)(2,1)S(1)} custom-call(s32[28,1,8]{2,1,0:T(1,128)S(1)} %bitcast.8, bf16[8,128,128]{2,1,0:T(8,128)(2,1)} %bitcast.10, bf16[8,128,128]{2,1,0:T(8,128)(2,1)} %bitcast.11, bf16[7,32,128,128]{3,2,1,0:T(8,128)(2,1)} %bitcast.9), custom_call_target="tpu_custom_call" | custom-call | tf_op jit(solution)/shard_map/pallas_call | solution.py:263
  61.1 0.7 %copy.7 = bf16[8,1,1,1,128,128]{5,4,3,2,1,0:T(8,128)(2,1)} copy(bf16[8,1,1,1,128,128]{5,4,3,2,1,0:T(8,128)(2,1)S(1)} %bitcast.7) | data formatting | bytes 524288
Async XLA Ops:
  0.0 0.7 %copy-start = (s32[7,1,1,4,1,8]{5,4,3,2,1,0:T(1,128)S(1)}, s32[7,1,1,4,1,8]{5,4,3,2,1,0:T(1,128)}, u32[]{:S(2)}) copy-start(s32[7,1,1,4,1,8]{5,4,3,2,1,0:T(1,128)} %param.7) | copy-start | bytes 2692

commit v5 on v4

--- a/solution.py
+++ b/solution.py
@@ -245,10 +245,11 @@
             out[l] = dot_nt(inv[l], jnp.concatenate(pieces, axis=0)).astype(BF16)
         if l + 2 < levels:
             deferred(l + 2, 0, l)
-
-    for l in range(steps):
-        waiting(xs.at[l, :, pl.ds(0, rows - 1)], xsend.at[l])
-        waiting(part_out.at[l], psend.at[l])
+        waiting(xs.at[l - 1, :, pl.ds(0, rows - 1)], xsend.at[l - 1])
+        if l < steps:
+            waiting(part_out.at[l - 1], psend.at[l - 1])
+
+    waiting(part_out.at[steps - 1], psend.at[steps - 1])
 
 
 def body(rows, cols, right_sides, inverses, blocks, targets):

time: 62 us -> 62 us (level)
  no operation moved by 1% of the time
where the time goes in v5:
time: 62 us; the launch traced here: 61.8 us
  Pallas kernels  60.3 us (97%)
  local copies, waits for them, and re-layouts  1.42 us (2%)
    pallas_call x1, Pallas kernels, body(): pl.pallas_call(functools.partial(kernel, (levels, rows, cols, nbr, size,...  60.3 us
    unnamed x3, local copies, waits for them, and re-layouts  1.42 us

profile of v5, /device:TPU:0, one launch (start us, length us, event | category | flops | bytes accessed | tf_op | source)
XLA Modules:
  0.0 61.8 jit_solution(6769326701674278323)
XLA Ops:
  0.0 0.0 copy-start
  0.0 0.7 %copy-done = s32[7,1,1,4,1,8]{5,4,3,2,1,0:T(1,128)S(1)} copy-done((s32[7,1,1,4,1,8]{5,4,3,2,1,0:T(1,128)S(1)}, s32[7,1,1,4,1,8]{5,4,3,2,1,0:T(1,128)}, u32[]{:S(2)}) %copy-start) | copy-done | bytes 920
  0.7 60.3 %shard_map.46 = bf16[8,128,128]{2,1,0:T(8,128)(2,1)S(1)} custom-call(s32[28,1,8]{2,1,0:T(1,128)S(1)} %bitcast.8, bf16[8,128,128]{2,1,0:T(8,128)(2,1)} %bitcast.10, bf16[8,128,128]{2,1,0:T(8,128)(2,1)} %bitcast.11, bf16[7,32,128,128]{3,2,1,0:T(8,128)(2,1)} %bitcast.9), custom_call_target="tpu_custom_call" | custom-call | tf_op jit(solution)/shard_map/pallas_call | solution.py:264
  61.1 0.7 %copy.7 = bf16[8,1,1,1,128,128]{5,4,3,2,1,0:T(8,128)(2,1)} copy(bf16[8,1,1,1,128,128]{5,4,3,2,1,0:T(8,128)(2,1)S(1)} %bitcast.7) | data formatting | bytes 524288
Async XLA Ops:
  0.0 0.7 %copy-start = (s32[7,1,1,4,1,8]{5,4,3,2,1,0:T(1,128)S(1)}, s32[7,1,1,4,1,8]{5,4,3,2,1,0:T(1,128)}, u32[]{:S(2)}) copy-start(s32[7,1,1,4,1,8]{5,4,3,2,1,0:T(1,128)} %param.7) | copy-start | bytes 2692

commit v6 on v5

--- a/solution.py
+++ b/solution.py
@@ -9,7 +9,7 @@
 
 MESH = pl.DeviceIdType.MESH
 CHUNKS = 4
-GROUP = 4
+GROUP = 8
 F32 = jnp.float32
 BF16 = jnp.bfloat16
 
@@ -180,16 +180,19 @@
     def partials(l, h):
         lhs = lhs_of(l - 1, h)
         at = pl.ds(h * half, half)
-        for k in col_order + [0]:
-            value = dot_nt(lhs, factor(l, col_peer[k], l - 1))
-            if l >= 2:
-                value = value + acc[l % 2, k, at, :]
-            if k:
-                part_out[l - 1, h, k - 1] = value.astype(BF16)
-            else:
-                own[h] = value
-        for k in col_order:
-            p_copy(l, h, k).start()
+        ks = col_order + [0]
+        for batch in (ks[: cols // 2], ks[cols // 2 :]):
+            for k in batch:
+                value = dot_nt(lhs, factor(l, col_peer[k], l - 1))
+                if l >= 2:
+                    value = value + acc[l % 2, k, at, :]
+                if k:
+                    part_out[l - 1, h, k - 1] = value.astype(BF16)
+                else:
+                    own[h] = value
+            for k in batch:
+                if k:
+                    p_copy(l, h, k).start()
 
     def send(l, h, value):
         xs[l, h, r] = value

time: 62 us -> 61.8 us (level)
  no operation moved by 1% of the time
where the time goes in v6:
time: 61.8 us; the launch traced here: 61.6 us
  Pallas kernels  60.1 us (97%)
  local copies, waits for them, and re-layouts  1.42 us (2%)
    pallas_call x1, Pallas kernels, body(): pl.pallas_call(functools.partial(kernel, (levels, rows, cols, nbr, size,...  60.1 us
    unnamed x3, local copies, waits for them, and re-layouts  1.42 us

profile of v6, /device:TPU:0, one launch (start us, length us, event | category | flops | bytes accessed | tf_op | source)
XLA Modules:
  0.0 61.6 jit_solution(6404700474509721246)
XLA Ops:
  0.0 0.0 copy-start
  0.0 0.7 %copy-done = s32[7,1,1,4,1,8]{5,4,3,2,1,0:T(1,128)S(1)} copy-done((s32[7,1,1,4,1,8]{5,4,3,2,1,0:T(1,128)S(1)}, s32[7,1,1,4,1,8]{5,4,3,2,1,0:T(1,128)}, u32[]{:S(2)}) %copy-start) | copy-done | bytes 920
  0.7 60.1 %shard_map.46 = bf16[8,128,128]{2,1,0:T(8,128)(2,1)S(1)} custom-call(s32[28,1,8]{2,1,0:T(1,128)S(1)} %bitcast.8, bf16[8,128,128]{2,1,0:T(8,128)(2,1)} %bitcast.10, bf16[8,128,128]{2,1,0:T(8,128)(2,1)} %bitcast.11, bf16[7,32,128,128]{3,2,1,0:T(8,128)(2,1)} %bitcast.9), custom_call_target="tpu_custom_call" | custom-call | tf_op jit(solution)/shard_map/pallas_call | solution.py:267
  60.9 0.7 %copy.7 = bf16[8,1,1,1,128,128]{5,4,3,2,1,0:T(8,128)(2,1)} copy(bf16[8,1,1,1,128,128]{5,4,3,2,1,0:T(8,128)(2,1)S(1)} %bitcast.7) | data formatting | bytes 524288
Async XLA Ops:
  0.0 0.7 %copy-start = (s32[7,1,1,4,1,8]{5,4,3,2,1,0:T(1,128)S(1)}, s32[7,1,1,4,1,8]{5,4,3,2,1,0:T(1,128)}, u32[]{:S(2)}) copy-start(s32[7,1,1,4,1,8]{5,4,3,2,1,0:T(1,128)} %param.7) | copy-start | bytes 2692
